TPU v7x, 32 devices: a whole 2x2x4 slice. The times are simulated.
32 devices in a mesh: dp: 2 (over y), seq: 16 (over z, x, core).
Axes of the slice: x: 2, y: 2, z: 4, core: 2. Of those that a mesh axis runs over, the one named last changes fastest.
Arguments:
- signal: bfloat16 [8, 4, 512, 512], P(None, 'dp', 'seq'), may hold values from -6 to 6
- cotangent: bfloat16 [8, 4, 512, 512], P(None, 'dp', 'seq'), may hold values from -6 to 6
- filter_spec: bfloat16 [2, 8, 512, 512], P(None, None, 'seq'), may hold values from -4.1875 to 4.1875
Outputs:
- output: bfloat16 [8, 4, 512, 512], P(None, 'dp', 'seq')
- grad_signal: bfloat16 [8, 4, 512, 512], P(None, 'dp', 'seq')
- grad_filter: bfloat16 [2, 8, 512, 512], P(None, None, 'seq')
All inputs are finite; a program needn't handle non-finite values.
Results may differ from a plain program's by a relative error of at most 0.0091.
Values may be sent and summed in bfloat16 or wider, within the bound.
A program may use at most 64 MiB of HBM per device.

v0:
```python
import math

import jax
import jax.numpy as jnp
from jax import lax
from jax.sharding import PartitionSpec as P

NB = 512


def unit_tables(block_size):
    steps_index = jnp.arange(block_size, dtype=jnp.int32)
    product_index = steps_index[:, None] * steps_index[None, :] % block_size
    phases = product_index.astype(jnp.float32) * (2.0 * math.pi / block_size)
    factor = 1.0 / math.sqrt(block_size)
    return (
        (jnp.cos(phases) * factor).astype(jnp.bfloat16),
        (-jnp.sin(phases) * factor).astype(jnp.bfloat16),
    )


def twiddle(row_index, col_index, length_all, orient):
    phases = (row_index[:, None] * col_index[None, :]).astype(jnp.float32) * (
        orient * 2.0 * math.pi / length_all
    )
    return (jnp.cos(phases), jnp.sin(phases))


def forward_rows(signal, tables, first_row, length_all):
    big_cos, big_sin, small_cos, small_sin = tables
    real_part = jnp.einsum("ncrs,as->ncra", signal, big_cos, preferred_element_type=jnp.float32)
    imaginary = jnp.einsum("ncrs,as->ncra", signal, big_sin, preferred_element_type=jnp.float32)
    row_index = first_row + jnp.arange(signal.shape[2], dtype=jnp.int32)
    col_index = jnp.arange(signal.shape[3], dtype=jnp.int32)
    turn_cos, turn_sin = twiddle(row_index, col_index, length_all, -1.0)
    middle = jnp.stack(
        [real_part * turn_cos - imaginary * turn_sin, real_part * turn_sin + imaginary * turn_cos]
    ).astype(jnp.bfloat16)
    received = lax.all_to_all(middle, "seq", split_axis=4, concat_axis=3, tiled=True)
    real_received = received[0]
    imaginary_received = received[1]
    out_real = jnp.einsum(
        "ncra,qr->ncaq", real_received, small_cos, preferred_element_type=jnp.float32
    ) - jnp.einsum(
        "ncra,qr->ncaq", imaginary_received, small_sin, preferred_element_type=jnp.float32
    )
    out_imaginary = jnp.einsum(
        "ncra,qr->ncaq", imaginary_received, small_cos, preferred_element_type=jnp.float32
    ) + jnp.einsum("ncra,qr->ncaq", real_received, small_sin, preferred_element_type=jnp.float32)
    return jnp.stack([out_real, out_imaginary])


def inverse_rows(spectrum, tables, first_freq, length_all):
    big_cos, big_sin, small_cos, small_sin = tables
    real_part = jnp.einsum(
        "ncaq,rq->ncar", spectrum[0], small_cos, preferred_element_type=jnp.float32
    ) + jnp.einsum("ncaq,rq->ncar", spectrum[1], small_sin, preferred_element_type=jnp.float32)
    imaginary = jnp.einsum(
        "ncaq,rq->ncar", spectrum[1], small_cos, preferred_element_type=jnp.float32
    ) - jnp.einsum("ncaq,rq->ncar", spectrum[0], small_sin, preferred_element_type=jnp.float32)
    row_index = first_freq + jnp.arange(spectrum.shape[3], dtype=jnp.int32)
    col_index = jnp.arange(spectrum.shape[4], dtype=jnp.int32)
    turn_cos, turn_sin = twiddle(row_index, col_index, length_all, 1.0)
    middle = jnp.stack(
        [real_part * turn_cos - imaginary * turn_sin, real_part * turn_sin + imaginary * turn_cos]
    ).astype(jnp.bfloat16)
    received = lax.all_to_all(middle, "seq", split_axis=4, concat_axis=3, tiled=True)
    total = jnp.einsum(
        "ncar,sa->ncrs", received[0], big_cos, preferred_element_type=jnp.float32
    ) + jnp.einsum("ncar,sa->ncrs", received[1], big_sin, preferred_element_type=jnp.float32)
    return total.astype(jnp.bfloat16)


def body(signal, cotangent, filter_spec):
    rows_total = signal.shape[2] * lax.axis_size("seq")
    big_cos, big_sin = unit_tables(NB)
    small_cos, small_sin = unit_tables(rows_total)
    tables = (big_cos, big_sin, small_cos, small_sin)
    length_all = NB * rows_total
    first_row = lax.axis_index("seq") * signal.shape[2]
    first_freq = lax.axis_index("seq") * (NB // lax.axis_size("seq"))
    filter_real = filter_spec[0].astype(jnp.float32)[:, None]
    filter_imaginary = filter_spec[1].astype(jnp.float32)[:, None]
    channels = signal.shape[1]
    stacked = forward_rows(
        jnp.concatenate([signal, cotangent], axis=1), tables, first_row, length_all
    )
    signal_spec = stacked[:, :, :channels]
    cotangent_spec = stacked[:, :, channels:]
    joined_input = jnp.concatenate(
        [
            jnp.stack(
                [
                    filter_real * signal_spec[0] - filter_imaginary * signal_spec[1],
                    filter_real * signal_spec[1] + filter_imaginary * signal_spec[0],
                ]
            ).astype(jnp.bfloat16),
            jnp.stack(
                [
                    filter_real * cotangent_spec[0] + filter_imaginary * cotangent_spec[1],
                    filter_real * cotangent_spec[1] - filter_imaginary * cotangent_spec[0],
                ]
            ).astype(jnp.bfloat16),
        ],
        axis=2,
    )
    results = inverse_rows(joined_input, tables, first_freq, length_all)
    output = results[:, :channels]
    grad_signal = results[:, channels:]
    grad_terms = jnp.stack(
        [
            jnp.sum(
                cotangent_spec[0] * signal_spec[0] + cotangent_spec[1] * signal_spec[1], axis=1
            ),
            jnp.sum(
                cotangent_spec[1] * signal_spec[0] - cotangent_spec[0] * signal_spec[1], axis=1
            ),
        ]
    )
    grad_filter = lax.psum(grad_terms, "dp")
    return (output, grad_signal, grad_filter.astype(jnp.bfloat16))


def solution(mesh):
    placed = (P(None, "dp", "seq", None), P(None, "dp", "seq", None), P(None, None, "seq", None))
    return jax.shard_map(
        body,
        mesh=mesh,
        in_specs=placed,
        out_specs=(
            P(None, "dp", "seq", None),
            P(None, "dp", "seq", None),
            P(None, None, "seq", None),
        ),
        check_vma=False,
    )
```

profile of v0, /device:TPU:11, one launch (start us, length us, event | category | flops | bytes accessed | tf_op | source)
XLA Modules:
  0.0 308.2 jit_solution(8221214854444377996)
XLA Ops:
  3.4 5.7 %fusion.19 = f32[8,4,32,512]{3,2,1,0:T(8,128)S(1)} fusion(bf16[8,4,32,512]{3,2,1,0:T(8,128)(2,1)S(1)} %constant_dynamic-update-slice_fusion), kind=kOutput, calls=%fused_computation.42 | convolution fusion | flops 541327360 | bytes 3145728 | tf_op jit(solution)/shard_map/ncrs,as->ncra/dot_general | solution.py:32
  9.1 5.6 %fusion.3 = (bf16[1,8,4,32,512]{4,3,2,1,0:T(8,128)(2,1)S(1)}, bf16[1,8,4,32,512]{4,3,2,1,0:T(8,128)(2,1)S(1)}) fusion(f32[8,4,32,512]{3,2,1,0:T(8,128)S(1)} %fusion.19, f32[32,512]{1,0:T(8,128)S(1)} %get-tuple-element.26, f32[32,512]{1,0:T(8,128)S(1)} %get-tuple-element.28, bf16[8,4,32,512]{3,2,1,0:T(8,128)(2,1)S(1)} %constant_dynamic-update-slice_fusion), kind=kOutput, calls=%fused_computation.20 | convolution fusion | flops 545259520 | bytes 5373952 | tf_op jit(solution)/shard_map/ncrs,as->ncra/dot_general | solution.py:31
  14.8 10.6 %copy.10 = bf16[2,8,4,32,512]{3,2,1,0,4:T(4,128)(2,1)} copy(bf16[2,8,4,32,512]{4,3,2,1,0:T(8,128)(2,1)S(1)} %pad_maximum_fusion) | data formatting | bytes 4194304 | tf_op jit(solution)/shard_map/stack | solution.py:36
  25.4 14.5 %reshape.119 = bf16[16,2,32768]{2,1,0:T(2,128)(2,1)} reshape(bf16[512,2,8,4,32]{4,3,2,1,0:T(4,128)(2,1)} %bitcast.90) | data formatting | bytes 4194304
  39.9 6.9 %all-to-all-start = ((bf16[16,2,32768]{2,1,0:T(2,128)(2,1)}), bf16[16,2,32768]{2,1,0:T(2,128)(2,1)S(1)}, u32[]{:S(2)}, u32[]{:S(2)}) async-start(bf16[16,2,32768]{2,1,0:T(2,128)(2,1)} %reshape.119), calls=%async_computation | async-start | bytes 4194304 | tf_op jit(solution)/shard_map/all_to_all | solution.py:39
  47.9 46.2 %all-to-all-done = bf16[16,2,32768]{2,1,0:T(2,128)(2,1)S(1)} async-done(((bf16[16,2,32768]{2,1,0:T(2,128)(2,1)}), bf16[16,2,32768]{2,1,0:T(2,128)(2,1)S(1)}, u32[]{:S(2)}, u32[]{:S(2)}) %all-to-all-start) | async-done | bytes 2097184 | tf_op jit(solution)/shard_map/all_to_all | solution.py:39
  94.0 8.8 %reshape.120 = bf16[512,2,8,4,32]{4,3,2,1,0:T(4,128)(2,1)} reshape(bf16[16,2,32768]{2,1,0:T(2,128)(2,1)S(1)} %all-to-all-done) | data formatting | bytes 4194304
  102.8 12.0 %copy.19 = bf16[2,8,4,32,16,32]{3,4,5,2,1,0:T(8,128)(2,1)} copy(bf16[2,8,4,32,16,32]{3,2,1,0,5,4:T(4,128)(2,1)} %bitcast.92) | data formatting | bytes 4194304 | tf_op jit(solution)/shard_map/all_to_all | solution.py:39
  114.8 6.6 %fusion.96 = (bf16[1,8,4,16,32,32]{4,3,5,2,1,0:T(8,128)(2,1)}, bf16[1,8,4,16,32,32]{4,3,5,2,1,0:T(8,128)(2,1)}) fusion(bf16[2,8,4,16,32,32]{4,3,5,2,1,0:T(8,128)(2,1)} %bitcast.94), kind=kLoop, calls=%fused_computation.120 | loop fusion | bytes 4194304 | tf_op jit(solution)/shard_map/slice | solution.py:40
  121.4 5.9 %squeeze.12 = bf16[8,4,512,32]{2,3,1,0:T(8,128)(2,1)S(1)} reshape(bf16[1,8,4,16,32,32]{4,3,5,2,1,0:T(8,128)(2,1)} %get-tuple-element.7) | data formatting | bytes 2097152 | tf_op jit(solution)/shard_map/squeeze | solution.py:40
  127.3 6.4 %fusion.27 = f32[8,4,32,512]{3,2,1,0:T(8,128)} fusion(bf16[8,4,512,32]{2,3,1,0:T(8,128)(2,1)S(1)} %squeeze.12), kind=kOutput, calls=%fused_computation.45 | convolution fusion | flops 541065216 | bytes 3145728 | tf_op jit(solution)/shard_map/ncra,qr->ncaq/dot_general | solution.py:42
  133.7 5.9 %squeeze.13 = bf16[8,4,512,32]{2,3,1,0:T(8,128)(2,1)S(1)} reshape(bf16[1,8,4,16,32,32]{4,3,5,2,1,0:T(8,128)(2,1)} %get-tuple-element.8) | data formatting | bytes 2097152 | tf_op jit(solution)/shard_map/squeeze | solution.py:41
  139.6 6.0 %fusion.25 = f32[8,4,32,512]{3,2,1,0:T(8,128)S(1)} fusion(bf16[8,4,512,32]{2,3,1,0:T(8,128)(2,1)S(1)} %squeeze.13), kind=kOutput, calls=%fused_computation.44 | convolution fusion | flops 541065216 | bytes 3145728 | tf_op jit(solution)/shard_map/ncra,qr->ncaq/dot_general | solution.py:47
  145.7 6.1 %subtract_bitcast_fusion = f32[1,8,4,32,512]{4,3,2,1,0:T(8,128)S(1)} fusion(f32[8,4,32,512]{3,2,1,0:T(8,128)S(1)} %copy-done, bf16[8,4,512,32]{2,3,1,0:T(8,128)(2,1)S(1)} %squeeze.13), kind=kOutput, calls=%fused_computation.9 | convolution fusion | flops 541851648 | bytes 5242880 | tf_op jit(solution)/shard_map/ncra,qr->ncaq/dot_general | solution.py:44
  151.8 6.3 %add_bitcast_fusion = f32[1,8,4,32,512]{4,3,2,1,0:T(8,128)S(1)} fusion(f32[8,4,32,512]{3,2,1,0:T(8,128)S(1)} %fusion.25, bf16[8,4,512,32]{2,3,1,0:T(8,128)(2,1)S(1)} %squeeze.12), kind=kOutput, calls=%fused_computation.8 | convolution fusion | flops 541851648 | bytes 5242880 | tf_op jit(solution)/shard_map/ncra,qr->ncaq/dot_general | solution.py:49
  158.1 1.9 add_reduce_fusion
  160.1 4.4 %fusion.11 = f32[8,4,32,512]{3,2,1,0:T(8,128)S(1)} fusion(bf16[2,8,4,32,512]{4,3,2,1,0:T(8,128)(2,1)S(1)} %maximum_maximum_fusion), kind=kOutput, calls=%fused_computation.39 | convolution fusion | flops 541065216 | bytes 3145728 | tf_op jit(solution)/shard_map/ncaq,rq->ncar/dot_general | solution.py:58
  164.5 4.4 %fusion.10 = f32[8,4,32,512]{3,2,1,0:T(8,128)S(1)} fusion(bf16[2,8,4,32,512]{4,3,2,1,0:T(8,128)(2,1)S(1)} %maximum_maximum_fusion), kind=kOutput, calls=%fused_computation.38 | convolution fusion | flops 541065216 | bytes 3145728 | tf_op jit(solution)/shard_map/ncaq,rq->ncar/dot_general | solution.py:55
  168.9 4.6 %convolution_subtract_fusion = f32[8,4,32,512]{3,2,1,0:T(8,128)S(1)} fusion(f32[8,4,32,512]{3,2,1,0:T(8,128)S(1)} %fusion.11, bf16[2,8,4,32,512]{4,3,2,1,0:T(8,128)(2,1)S(1)} %maximum_maximum_fusion), kind=kOutput, calls=%fused_computation.12 | convolution fusion | flops 541851648 | bytes 5242880 | tf_op jit(solution)/shard_map/ncaq,rq->ncar/dot_general | solution.py:60
  173.6 5.0 %fusion.5 = (bf16[1,8,4,32,512]{4,3,2,1,0:T(8,128)(2,1)S(1)}, bf16[1,8,4,32,512]{4,3,2,1,0:T(8,128)(2,1)S(1)}) fusion(f32[8,4,32,512]{3,2,1,0:T(8,128)S(1)} %convolution_subtract_fusion, f32[32,512]{1,0:T(8,128)S(1)} %get-tuple-element.27, f32[32,512]{1,0:T(8,128)S(1)} %get-tuple-element.25, f32[8,4,32,512]{3,2,1,0:T(8,128)S(1)} %fusion.10, ...), kind=kOutput, calls=%fused_computation.22 | convolution fusion | flops 546045952 | bytes 7471104 | tf_op jit(solution)/shard_map/ncaq,rq->ncar/dot_general | solution.py:57
  178.7 10.6 %copy.12 = bf16[2,8,4,32,512]{3,2,1,0,4:T(4,128)(2,1)} copy(bf16[2,8,4,32,512]{4,3,2,1,0:T(8,128)(2,1)S(1)} %pad_maximum_fusion.1) | data formatting | bytes 4194304 | tf_op jit(solution)/shard_map/stack | solution.py:64
  189.3 14.5 %reshape.121 = bf16[16,2,32768]{2,1,0:T(2,128)(2,1)} reshape(bf16[512,2,8,4,32]{4,3,2,1,0:T(4,128)(2,1)} %bitcast.91) | data formatting | bytes 4194304
  203.8 4.9 %all-to-all-start.1 = ((bf16[16,2,32768]{2,1,0:T(2,128)(2,1)}), bf16[16,2,32768]{2,1,0:T(2,128)(2,1)S(1)}, u32[]{:S(2)}, u32[]{:S(2)}) async-start(bf16[16,2,32768]{2,1,0:T(2,128)(2,1)} %reshape.121), calls=%async_computation.1 | async-start | bytes 4194304 | tf_op jit(solution)/shard_map/all_to_all | solution.py:67
  210.0 28.6 %all-reduce.1 = bf16[2,8,32,512]{3,2,1,0:T(8,128)(2,1)} all-reduce(f32[2,8,32,512]{3,2,1,0:T(8,128)S(1)} %pad_maximum_fusion.2), channel_id=1, replica_groups=mesh['dp'=2,'seq'=16] {'dp'}, use_global_device_ids=true, to_apply=%region_2.3 | all-reduce | flops 262144 | bytes 1572864 | tf_op jit(solution)/shard_map/psum | solution.py:120
  238.6 17.5 %all-to-all-done.1 = bf16[16,2,32768]{2,1,0:T(2,128)(2,1)S(1)} async-done(((bf16[16,2,32768]{2,1,0:T(2,128)(2,1)}), bf16[16,2,32768]{2,1,0:T(2,128)(2,1)S(1)}, u32[]{:S(2)}, u32[]{:S(2)}) %all-to-all-start.1) | async-done | bytes 2097184 | tf_op jit(solution)/shard_map/all_to_all | solution.py:67
  256.1 8.8 %reshape.122 = bf16[512,2,8,4,32]{4,3,2,1,0:T(4,128)(2,1)} reshape(bf16[16,2,32768]{2,1,0:T(2,128)(2,1)S(1)} %all-to-all-done.1) | data formatting | bytes 4194304
  264.9 12.0 %copy.18 = bf16[2,8,4,32,16,32]{3,4,5,2,1,0:T(8,128)(2,1)} copy(bf16[2,8,4,32,16,32]{3,2,1,0,5,4:T(4,128)(2,1)} %bitcast.93) | data formatting | bytes 4194304 | tf_op jit(solution)/shard_map/all_to_all | solution.py:67
  276.9 6.6 %fusion.95 = (bf16[1,8,4,16,32,32]{4,3,5,2,1,0:T(8,128)(2,1)}, bf16[1,8,4,16,32,32]{4,3,5,2,1,0:T(8,128)(2,1)}) fusion(bf16[2,8,4,16,32,32]{4,3,5,2,1,0:T(8,128)(2,1)} %bitcast.95), kind=kLoop, calls=%fused_computation.119 | loop fusion | bytes 4194304 | tf_op jit(solution)/shard_map/slice | solution.py:70
  283.4 5.9 %squeeze.16 = bf16[8,4,512,32]{2,3,1,0:T(8,128)(2,1)S(1)} reshape(bf16[1,8,4,16,32,32]{4,3,5,2,1,0:T(8,128)(2,1)} %get-tuple-element.6) | data formatting | bytes 2097152 | tf_op jit(solution)/shard_map/squeeze | solution.py:69
  289.4 5.6 %fusion.21 = f32[8,4,32,512]{3,2,1,0:T(8,128)S(1)} fusion(bf16[8,4,512,32]{2,3,1,0:T(8,128)(2,1)S(1)} %squeeze.16), kind=kOutput, calls=%fused_computation.43 | convolution fusion | flops 541065216 | bytes 3145728 | tf_op jit(solution)/shard_map/ncar,sa->ncrs/dot_general | solution.py:68
  295.0 6.2 %squeeze.17 = bf16[8,4,512,32]{2,3,1,0:T(8,128)(2,1)S(1)} reshape(bf16[1,8,4,16,32,32]{4,3,5,2,1,0:T(8,128)(2,1)} %get-tuple-element.5) | data formatting | bytes 2097152 | tf_op jit(solution)/shard_map/squeeze | solution.py:70
  301.2 5.6 %add_convert_fusion = bf16[8,4,32,512]{3,2,1,0:T(8,128)(2,1)S(1)} fusion(f32[8,4,32,512]{3,2,1,0:T(8,128)S(1)} %fusion.21, bf16[8,4,512,32]{2,3,1,0:T(8,128)(2,1)S(1)} %squeeze.17), kind=kOutput, calls=%fused_computation.5 | convolution fusion | flops 542375936 | bytes 4194304 | tf_op jit(solution)/shard_map/ncar,sa->ncrs/dot_general | solution.py:70
  (12 shorter events, 6.8 us)
Async XLA Ops:
  39.9 54.2 %all-to-all-start = ((bf16[16,2,32768]{2,1,0:T(2,128)(2,1)}), bf16[16,2,32768]{2,1,0:T(2,128)(2,1)S(1)}, u32[]{:S(2)}, u32[]{:S(2)}) async-start(bf16[16,2,32768]{2,1,0:T(2,128)(2,1)} %reshape.119), calls=%async_computation | async-start | bytes 4194304 | tf_op jit(solution)/shard_map/all_to_all | solution.py:39
  139.6 6.1 %copy-start = (f32[8,4,32,512]{3,2,1,0:T(8,128)S(1)}, f32[8,4,32,512]{3,2,1,0:T(8,128)}, u32[]{:S(2)}) copy-start(f32[8,4,32,512]{3,2,1,0:T(8,128)} %fusion.27) | copy-start | bytes 6291460
  203.8 52.3 %all-to-all-start.1 = ((bf16[16,2,32768]{2,1,0:T(2,128)(2,1)}), bf16[16,2,32768]{2,1,0:T(2,128)(2,1)S(1)}, u32[]{:S(2)}, u32[]{:S(2)}) async-start(bf16[16,2,32768]{2,1,0:T(2,128)(2,1)} %reshape.121), calls=%async_computation.1 | async-start | bytes 4194304 | tf_op jit(solution)/shard_map/all_to_all | solution.py:67
where the time goes:
time: 314 us; the launch traced here: 308 us
  local copies, waits for them, and re-layouts  132 us (42%)
  matrix products  65.6 us (21%)
  waiting for transfers between devices  63.6 us (20%)
  blocking collectives  28.6 us (9%)
  starting transfers between devices  11.8 us (4%)
  other arithmetic  5.41 us (2%)
    unnamed x7, local copies, waits for them, and re-layouts  47.6 us
    all_to_all x1, waiting for transfers between devices, forward_rows(): lax.all_to_all(middle, 'seq', split_axis=4, concat_axis=3, tiled=True)  46.2 us
    psum x1, blocking collectives, body(): grad_filter = lax.psum(grad_terms, 'dp')  28.6 us
    all_to_all x1, waiting for transfers between devices, inverse_rows(): lax.all_to_all(middle, 'seq', split_axis=4, concat_axis=3, tiled=True)  17.5 us
    all_to_all x1, local copies, waits for them, and re-layouts, forward_rows(): lax.all_to_all(middle, 'seq', split_axis=4, concat_axis=3, tiled=True)  12 us
    all_to_all x1, local copies, waits for them, and re-layouts, inverse_rows(): lax.all_to_all(middle, 'seq', split_axis=4, concat_axis=3, tiled=True)  12 us
    another operation x1, local copies, waits for them, and re-layouts, inverse_rows(): jnp.stack([real_part * turn_cos - imaginary * turn_sin, real_part * turn_...  10.6 us
    another operation x1, local copies, waits for them, and re-layouts, forward_rows(): jnp.stack([real_part * turn_cos - imaginary * turn_sin, real_part * turn_...  10.6 us
  transfers between devices with their start and end apart: 2, of which 2 were waited for; matrix products, arithmetic and copies ran while one was open for 1% of the time, Pallas kernels for 0%

commit v1 on v0

--- a/solution.py
+++ b/solution.py
@@ -1,9 +1,15 @@
+import functools
 import math
 
 import jax
 import jax.numpy as jnp
+import numpy as np
 from jax import lax
+from jax.experimental import pallas as pl
+from jax.experimental.pallas import tpu as pltpu
 from jax.sharding import PartitionSpec as P
+
+MESH = pl.DeviceIdType.MESH
 
 NB = 512
 
@@ -121,16 +127,409 @@
     return (output, grad_signal, grad_filter.astype(jnp.bfloat16))
 
 
+def whole_tables(size):
+    index = np.arange(size)
+    phases = (index[:, None] * index[None, :] % size) * (2.0 * math.pi / size)
+    factor = 1.0 / math.sqrt(size)
+    cos_table, sin_table = np.cos(phases) * factor, -np.sin(phases) * factor
+    forward = np.block([[cos_table, sin_table], [-sin_table, cos_table]])
+    turn = (index[:, None] * index[None, :]) * (2.0 * math.pi / (size * size))
+    return (
+        forward.astype(jnp.bfloat16),
+        forward.T.astype(jnp.bfloat16),
+        np.cos(turn).astype(np.float32),
+        np.sin(turn).astype(np.float32),
+    )
+
+
+def whole_sequences_fit(mesh, signal, filter_spec):
+    filters, channels, rows, size = signal.shape
+    n = mesh.shape["seq"]
+    return (
+        mesh.shape["dp"] == 2
+        and channels == 2
+        and filters * channels == n
+        and rows * n == size
+        and filter_spec.shape[2] == rows
+        and filter_spec.shape[3] == size
+        and rows % 32 == 0
+        and size % 256 == 0
+    )
+
+
+def whole_kernel(
+    n,
+    signal_ref,
+    cotangent_ref,
+    filter_ref,
+    forward_ref,
+    inverse_ref,
+    cos_ref,
+    sin_ref,
+    output_ref,
+    grad_signal_ref,
+    grad_filter_ref,
+    signal_all,
+    cotangent_all,
+    filter_all,
+    forward_table,
+    inverse_table,
+    turn_cos,
+    turn_sin,
+    signal_spec,
+    cotangent_spec,
+    middle,
+    output_all,
+    grad_all,
+    terms_wide,
+    terms,
+    terms_got,
+    grad_part,
+    table_sem,
+    filter_send,
+    filter_got,
+    share_send,
+    share_got,
+    signal_send,
+    signal_got,
+    cotangent_send,
+    cotangent_got,
+    output_send,
+    output_got,
+    grad_send,
+    grad_got,
+    terms_send,
+    terms_recv,
+    part_send,
+    part_got,
+    swap_send,
+    swap_got,
+):
+    size = signal_all.shape[0]
+    rows = size // n
+    half = rows // 2
+    chunk = 256
+    chunks = size // chunk
+    per_chunk = chunk // rows
+    me = lax.axis_index("seq")
+    side = lax.axis_index("dp")
+    other = 1 - side
+    channel = lax.rem(me, 2)
+    group = lax.div(me, 2)
+    mate = me + 1 - 2 * channel
+    my_half = pl.ds(pl.multiple_of(channel * half, half), half)
+    my_rows = pl.ds(pl.multiple_of(me * rows, rows), rows)
+    partners = ((side, mate), (other, me), (other, mate))
+
+    table_copies = [
+        pltpu.make_async_copy(source, target, table_sem.at[i])
+        for i, (source, target) in enumerate(
+            (
+                (forward_ref, forward_table),
+                (inverse_ref, inverse_table),
+                (cos_ref, turn_cos),
+                (sin_ref, turn_sin),
+            )
+        )
+    ]
+    for copy in table_copies:
+        copy.start()
+
+    barrier = pltpu.get_barrier_semaphore()
+
+    def greet(k, carry):
+        pl.semaphore_signal(
+            barrier, inc=1, device_id={"dp": side, "seq": lax.rem(me + k, n)}, device_id_type=MESH
+        )
+        return carry
+
+    lax.fori_loop(1, n, greet, 0)
+    for to_side, to_seq in partners[1:]:
+        pl.semaphore_signal(
+            barrier, inc=1, device_id={"dp": to_side, "seq": to_seq}, device_id_type=MESH
+        )
+    pl.semaphore_wait(barrier, n + 1)
+
+    def send_all(source_of, target, send_sem, recv_sem):
+        pltpu.make_async_copy(source_of(me), target, recv_sem).start()
+
+        def one(k, carry):
+            to = lax.rem(me + k, n)
+            pltpu.make_async_remote_copy(
+                src_ref=source_of(to),
+                dst_ref=target,
+                send_sem=send_sem,
+                recv_sem=recv_sem,
+                device_id={"dp": side, "seq": to},
+                device_id_type=MESH,
+            ).start()
+            return carry
+
+        lax.fori_loop(1, n, one, 0)
+
+    def wait_bytes(ref, sem):
+        pltpu.make_async_copy(ref, ref, sem).wait()
+
+    def filter_source(to):
+        start = pl.multiple_of(lax.rem(to, 2) * half, half)
+        return filter_ref.at[side, lax.div(to, 2), pl.ds(start, half), :]
+
+    pltpu.make_async_copy(
+        filter_source(me), filter_all.at[side, me, my_half, :], filter_got
+    ).start()
+
+    def send_filter(k, carry):
+        to = lax.rem(me + k, n)
+        start = pl.multiple_of(lax.rem(to, 2) * half, half)
+        pltpu.make_async_remote_copy(
+            src_ref=filter_source(to),
+            dst_ref=filter_all.at[side, me, pl.ds(start, half), :],
+            send_sem=filter_send,
+            recv_sem=filter_got,
+            device_id={"dp": side, "seq": to},
+            device_id_type=MESH,
+        ).start()
+        return carry
+
+    lax.fori_loop(1, n, send_filter, 0)
+    send_all(
+        lambda to: signal_ref.at[lax.div(to, 2), lax.rem(to, 2)],
+        signal_all.at[my_rows, :],
+        signal_send,
+        signal_got,
+    )
+    send_all(
+        lambda to: cotangent_ref.at[lax.div(to, 2), lax.rem(to, 2)],
+        cotangent_all.at[my_rows, :],
+        cotangent_send,
+        cotangent_got,
+    )
+
+    my_quarter = filter_all.at[side, :, my_half, :]
+    wait_bytes(my_quarter, filter_got)
+    share_copies = [
+        pltpu.make_async_remote_copy(
+            src_ref=my_quarter,
+            dst_ref=my_quarter,
+            send_sem=share_send.at[i],
+            recv_sem=share_got.at[i],
+            device_id={"dp": to_side, "seq": to_seq},
+            device_id_type=MESH,
+        )
+        for i, (to_side, to_seq) in enumerate(partners)
+    ]
+    for copy in share_copies:
+        copy.start()
+
+    for copy in table_copies:
+        copy.wait()
+
+    def transform(values, spec, i):
+        at = pl.ds(pl.multiple_of(i * chunk, chunk), chunk)
+        one_signal = values[...]
+        contract_last = (((1,), (1,)), ((), ()))
+        real = lax.dot_general(
+            forward_table[at, :size], one_signal, contract_last, preferred_element_type=jnp.float32
+        )
+        imaginary = lax.dot_general(
+            forward_table[at, size:], one_signal, contract_last, preferred_element_type=jnp.float32
+        )
+        cos_part, sin_part = turn_cos[at, :], turn_sin[at, :]
+        mid = jnp.concatenate(
+            [
+                (real * cos_part + imaginary * sin_part).astype(jnp.bfloat16),
+                (imaginary * cos_part - real * sin_part).astype(jnp.bfloat16),
+            ],
+            axis=1,
+        )
+        spec[at, :] = jnp.dot(mid, forward_table[...], preferred_element_type=jnp.float32)
+
+    def filtered(spec, sign, i):
+        at = pl.ds(pl.multiple_of(i * chunk, chunk), chunk)
+        blocks = pl.ds(i * per_chunk, per_chunk)
+        filter_real = filter_all[0, blocks].reshape(chunk, size).astype(jnp.float32)
+        filter_imaginary = filter_all[1, blocks].reshape(chunk, size).astype(jnp.float32) * sign
+        real, imaginary = spec[at, :size], spec[at, size:]
+        product = jnp.concatenate(
+            [
+                (filter_real * real - filter_imaginary * imaginary).astype(jnp.bfloat16),
+                (filter_real * imaginary + filter_imaginary * real).astype(jnp.bfloat16),
+            ],
+            axis=1,
+        )
+        both = jnp.dot(product, inverse_table[...], preferred_element_type=jnp.float32)
+        real, imaginary = both[:, :size], both[:, size:]
+        cos_part, sin_part = turn_cos[at, :], turn_sin[at, :]
+        middle[at, :] = (real * cos_part - imaginary * sin_part).astype(jnp.bfloat16)
+        below = pl.ds(pl.multiple_of(size + i * chunk, chunk), chunk)
+        middle[below, :] = (real * sin_part + imaginary * cos_part).astype(jnp.bfloat16)
+
+    def restored(result, i):
+        at = pl.ds(pl.multiple_of(i * chunk, chunk), chunk)
+        turned = jnp.dot(
+            forward_table[at, :], middle[...], preferred_element_type=jnp.float32
+        )
+        result[:, at] = turned.T.astype(jnp.bfloat16)
+
+    def loop(fn):
+        def one(i, carry):
+            fn(i)
+            return carry
+
+        lax.fori_loop(0, chunks, one, 0)
+
+    def rows_of(ref, to):
+        return ref.at[pl.ds(pl.multiple_of(to * rows, rows), rows), :]
+
+    wait_bytes(signal_all, signal_got)
+    loop(lambda i: transform(signal_all, signal_spec, i))
+    for copy in share_copies:
+        copy.wait()
+    loop(lambda i: filtered(signal_spec, 1.0, i))
+    loop(lambda i: restored(output_all, i))
+    send_all(
+        lambda to: rows_of(output_all, to), output_ref.at[group, channel], output_send, output_got
+    )
+
+    wait_bytes(cotangent_all, cotangent_got)
+
+    def transform_and_terms(i):
+        transform(cotangent_all, cotangent_spec, i)
+        at = pl.ds(pl.multiple_of(i * chunk, chunk), chunk)
+        blocks = pl.ds(i * per_chunk, per_chunk)
+        real, imaginary = signal_spec[at, :size], signal_spec[at, size:]
+        back_real, back_imaginary = cotangent_spec[at, :size], cotangent_spec[at, size:]
+        for part, values in enumerate(
+            (
+                back_real * real + back_imaginary * imaginary,
+                back_imaginary * real - back_real * imaginary,
+            )
+        ):
+            values = values.reshape(per_chunk, rows, size)
+            terms_wide[part, blocks] = values
+            terms[part, blocks] = values.astype(jnp.bfloat16)
+
+    loop(transform_and_terms)
+    terms_copies = []
+    for i, (to_side, to_seq) in enumerate(partners):
+        start = pl.multiple_of(lax.rem(to_seq, 2) * half, half)
+        terms_copies.append(
+            pltpu.make_async_remote_copy(
+                src_ref=terms.at[to_side, :, pl.ds(start, half), :],
+                dst_ref=terms_got.at[i],
+                send_sem=terms_send.at[i],
+                recv_sem=terms_recv.at[i],
+                device_id={"dp": to_side, "seq": to_seq},
+                device_id_type=MESH,
+            )
+        )
+    for copy in terms_copies:
+        copy.start()
+
+    loop(lambda i: filtered(cotangent_spec, -1.0, i))
+    loop(lambda i: restored(grad_all, i))
+    send_all(
+        lambda to: rows_of(grad_all, to), grad_signal_ref.at[group, channel], grad_send, grad_got
+    )
+
+    for copy in terms_copies:
+        copy.wait()
+    total = terms_wide[side, :, my_half, :]
+    for i in range(3):
+        total = total + terms_got[i].astype(jnp.float32)
+    grad_part[...] = total.astype(jnp.bfloat16)
+    send_all(
+        lambda to: grad_part.at[to],
+        grad_filter_ref.at[side, group, my_half, :],
+        part_send,
+        part_got,
+    )
+    wait_bytes(grad_filter_ref.at[side], part_got)
+    swap = pltpu.make_async_remote_copy(
+        src_ref=grad_filter_ref.at[side],
+        dst_ref=grad_filter_ref.at[side],
+        send_sem=swap_send,
+        recv_sem=swap_got,
+        device_id={"dp": other, "seq": me},
+        device_id_type=MESH,
+    )
+    swap.start()
+
+    wait_bytes(output_ref, output_got)
+    wait_bytes(grad_signal_ref, grad_got)
+    swap.wait()
+    sent = pl.ds(0, size - rows)
+    wait_bytes(signal_all.at[sent, :], signal_send)
+    wait_bytes(cotangent_all.at[sent, :], cotangent_send)
+    wait_bytes(output_all.at[sent, :], output_send)
+    wait_bytes(grad_all.at[sent, :], grad_send)
+    wait_bytes(grad_part.at[pl.ds(0, n - 1)], filter_send)
+    wait_bytes(grad_part.at[pl.ds(0, n - 1)], part_send)
+
+
+def whole_body(n, signal, cotangent, filter_spec):
+    size = signal.shape[3]
+    rows = signal.shape[2]
+    half = rows // 2
+    tables = [jnp.asarray(table) for table in whole_tables(size)]
+    bf16, f32 = jnp.bfloat16, jnp.float32
+    anywhere = pl.BlockSpec(memory_space=pl.ANY)
+    one_sem = pltpu.SemaphoreType.DMA(())
+    three = pltpu.SemaphoreType.DMA((3,))
+    return pl.pallas_call(
+        functools.partial(whole_kernel, n),
+        out_shape=tuple(
+            jax.ShapeDtypeStruct(x.shape, x.dtype) for x in (signal, cotangent, filter_spec)
+        ),
+        in_specs=[anywhere] * 7,
+        out_specs=(anywhere,) * 3,
+        scratch_shapes=[
+            pltpu.VMEM((size, size), bf16),
+            pltpu.VMEM((size, size), bf16),
+            pltpu.VMEM((2, n, rows, size), bf16),
+            pltpu.VMEM((2 * size, 2 * size), bf16),
+            pltpu.VMEM((2 * size, 2 * size), bf16),
+            pltpu.VMEM((size, size), f32),
+            pltpu.VMEM((size, size), f32),
+            pltpu.VMEM((size, 2 * size), f32),
+            pltpu.VMEM((size, 2 * size), f32),
+            pltpu.VMEM((2 * size, size), bf16),
+            pltpu.VMEM((size, size), bf16),
+            pltpu.VMEM((size, size), bf16),
+            pltpu.VMEM((2, n, rows, size), f32),
+            pltpu.VMEM((2, n, rows, size), bf16),
+            pltpu.VMEM((3, n, half, size), bf16),
+            pltpu.VMEM((n, half, size), bf16),
+            pltpu.SemaphoreType.DMA((4,)),
+            one_sem,
+            one_sem,
+            three,
+            three,
+        ]
+        + [one_sem] * 8
+        + [three, three]
+        + [one_sem] * 4,
+        compiler_params=pltpu.CompilerParams(
+            collective_id=0, has_side_effects=True, vmem_limit_bytes=44 * 1024 * 1024
+        ),
+        cost_estimate=pl.CostEstimate(
+            flops=24 * size**3 * 2, bytes_accessed=12 * size * size * 2, transcendentals=0
+        ),
+    )(signal, cotangent, filter_spec, *tables)
+
+
 def solution(mesh):
     placed = (P(None, "dp", "seq", None), P(None, "dp", "seq", None), P(None, None, "seq", None))
+
+    def step(signal, cotangent, filter_spec):
+        if whole_sequences_fit(mesh, signal, filter_spec):
+            return whole_body(mesh.shape["seq"], signal, cotangent, filter_spec)
+        return body(signal, cotangent, filter_spec)
+
     return jax.shard_map(
-        body,
+        step,
         mesh=mesh,
         in_specs=placed,
-        out_specs=(
-            P(None, "dp", "seq", None),
-            P(None, "dp", "seq", None),
-            P(None, None, "seq", None),
-        ),
+        out_specs=placed,
         check_vma=False,
     )

time: 314 us -> 85 us (0.27)
  the two profiles are of different devices: /device:TPU:11 before, /device:TPU:0 now
where the time goes in v1:
time: 85 us; the launch traced here: 84.5 us
  Pallas kernels  72.7 us (86%)
  local copies, waits for them, and re-layouts  11.1 us (13%)
    pallas_call x1, Pallas kernels, whole_body(): pl.pallas_call(functools.partial(whole_kernel, n), out_shape=tuple((jax.S...  72.7 us
    unnamed x17, local copies, waits for them, and re-layouts  11.1 us

profile of v1, /device:TPU:0, one launch (start us, length us, event | category | flops | bytes accessed | tf_op | source)
XLA Modules:
  0.0 84.5 jit_solution(10056811152548059730)
XLA Ops:
  0.6 0.0 copy-start
  0.6 1.0 %copy-done = bf16[8,2,32,512]{3,2,1,0:T(8,128)(2,1)S(1)} copy-done((bf16[8,2,32,512]{3,2,1,0:T(8,128)(2,1)S(1)}, bf16[8,2,32,512]{3,2,1,0:T(8,128)(2,1)}, u32[]{:S(2)}) %copy-start) | copy-done | bytes 524312
  1.7 0.0 copy-start.1
  1.7 1.0 %copy-done.1 = bf16[8,2,32,512]{3,2,1,0:T(8,128)(2,1)S(1)} copy-done((bf16[8,2,32,512]{3,2,1,0:T(8,128)(2,1)S(1)}, bf16[8,2,32,512]{3,2,1,0:T(8,128)(2,1)}, u32[]{:S(2)}) %copy-start.1) | copy-done | bytes 524312
  2.7 0.0 copy-start.2
  2.7 1.0 %copy-done.2 = bf16[2,8,32,512]{3,2,1,0:T(8,128)(2,1)S(1)} copy-done((bf16[2,8,32,512]{3,2,1,0:T(8,128)(2,1)S(1)}, bf16[2,8,32,512]{3,2,1,0:T(8,128)(2,1)}, u32[]{:S(2)}) %copy-start.2) | copy-done | bytes 524312
  3.8 0.0 copy-start.3
  3.8 1.6 %copy-done.3 = bf16[1024,1024]{1,0:T(8,128)(2,1)S(1)} copy-done((bf16[1024,1024]{1,0:T(8,128)(2,1)S(1)}, bf16[1024,1024]{1,0:T(8,128)(2,1)}, u32[]{:S(2)}) %copy-start.3) | copy-done | bytes 2097176
  5.3 0.0 copy-start.4
  5.4 1.6 %copy-done.4 = bf16[1024,1024]{1,0:T(8,128)(2,1)S(1)} copy-done((bf16[1024,1024]{1,0:T(8,128)(2,1)S(1)}, bf16[1024,1024]{1,0:T(8,128)(2,1)}, u32[]{:S(2)}) %copy-start.4) | copy-done | bytes 2097176
  6.9 0.0 copy-start.5
  6.9 1.2 %copy-done.5 = f32[512,512]{1,0:T(8,128)S(1)} copy-done((f32[512,512]{1,0:T(8,128)S(1)}, f32[512,512]{1,0:T(8,128)}, u32[]{:S(2)}) %copy-start.5) | copy-done | bytes 1048600
  8.2 0.0 copy-start.6
  8.2 1.2 %copy-done.6 = f32[512,512]{1,0:T(8,128)S(1)} copy-done((f32[512,512]{1,0:T(8,128)S(1)}, f32[512,512]{1,0:T(8,128)}, u32[]{:S(2)}) %copy-start.6) | copy-done | bytes 1048600
  9.4 72.7 %shard_map.94 = (bf16[8,2,32,512]{3,2,1,0:T(8,128)(2,1)S(1)}, bf16[8,2,32,512]{3,2,1,0:T(8,128)(2,1)S(1)}, bf16[2,8,32,512]{3,2,1,0:T(8,128)(2,1)S(1)}) custom-call(bf16[8,2,32,512]{3,2,1,0:T(8,128)(2,1)S(1)} %copy-done, bf16[8,2,32,512]{3,2,1,0:T(8,128)(2,1)S(1)} %copy-done.1, bf16[2,8,32,512]{3,2,1,0:T(8,128)(2,1)S(1)} %copy-done.2, ...), custom_call_target="tpu_custom_call" | custom-call | flops 6442450944 | bytes 6291456 | tf_op jit(solution)/shard_map/pallas_call | solution.py:479
  82.1 0.8 copy.13
  82.9 0.8 copy.14
  83.7 0.8 copy.15
Async XLA Ops:
  0.6 1.0 %copy-start = (bf16[8,2,32,512]{3,2,1,0:T(8,128)(2,1)S(1)}, bf16[8,2,32,512]{3,2,1,0:T(8,128)(2,1)}, u32[]{:S(2)}) copy-start(bf16[8,2,32,512]{3,2,1,0:T(8,128)(2,1)} %signal_ref.1) | copy-start | bytes 1572868
  1.7 1.0 %copy-start.1 = (bf16[8,2,32,512]{3,2,1,0:T(8,128)(2,1)S(1)}, bf16[8,2,32,512]{3,2,1,0:T(8,128)(2,1)}, u32[]{:S(2)}) copy-start(bf16[8,2,32,512]{3,2,1,0:T(8,128)(2,1)} %cotangent_ref.1) | copy-start | bytes 1572868
  2.7 1.0 %copy-start.2 = (bf16[2,8,32,512]{3,2,1,0:T(8,128)(2,1)S(1)}, bf16[2,8,32,512]{3,2,1,0:T(8,128)(2,1)}, u32[]{:S(2)}) copy-start(bf16[2,8,32,512]{3,2,1,0:T(8,128)(2,1)} %filter_ref.1) | copy-start | bytes 1572868
  3.8 1.6 %copy-start.3 = (bf16[1024,1024]{1,0:T(8,128)(2,1)S(1)}, bf16[1024,1024]{1,0:T(8,128)(2,1)}, u32[]{:S(2)}) copy-start(bf16[1024,1024]{1,0:T(8,128)(2,1)} %constant.9.clone.inverse_ref) | copy-start | bytes 6291460
  5.3 1.6 %copy-start.4 = (bf16[1024,1024]{1,0:T(8,128)(2,1)S(1)}, bf16[1024,1024]{1,0:T(8,128)(2,1)}, u32[]{:S(2)}) copy-start(bf16[1024,1024]{1,0:T(8,128)(2,1)} %constant.8.clone.forward_ref) | copy-start | bytes 6291460
  6.9 1.2 %copy-start.5 = (f32[512,512]{1,0:T(8,128)S(1)}, f32[512,512]{1,0:T(8,128)}, u32[]{:S(2)}) copy-start(f32[512,512]{1,0:T(8,128)} %constant.11.clone.sin_ref) | copy-start | bytes 3145732
  8.2 1.2 %copy-start.6 = (f32[512,512]{1,0:T(8,128)S(1)}, f32[512,512]{1,0:T(8,128)}, u32[]{:S(2)}) copy-start(f32[512,512]{1,0:T(8,128)} %constant.10.clone.cos_ref) | copy-start | bytes 3145732

commit v2 on v1

--- a/solution.py
+++ b/solution.py
@@ -182,7 +182,8 @@
     output_all,
     grad_all,
     terms_wide,
-    terms,
+    terms_mate,
+    terms_out,
     terms_got,
     grad_part,
     table_sem,
@@ -198,6 +199,8 @@
     output_got,
     grad_send,
     grad_got,
+    mate_send,
+    mate_got,
     terms_send,
     terms_recv,
     part_send,
@@ -250,11 +253,25 @@
         )
     pl.semaphore_wait(barrier, n + 1)
 
-    def send_all(source_of, target, send_sem, recv_sem):
-        pltpu.make_async_copy(source_of(me), target, recv_sem).start()
-
-        def one(k, carry):
-            to = lax.rem(me + k, n)
+    across = n // 2
+    my_part, place = lax.div(me, across), lax.rem(me, across)
+
+    def for_peers(first, last, send):
+        if first == 1:
+            send((1 - my_part) * across + place)
+
+        def one(t, carry):
+            part = lax.rem(my_part + lax.rem(t + me, 2), 2)
+            send(part * across + lax.rem(place + lax.div(t, 2), across))
+            return carry
+
+        lax.fori_loop(max(first, 2), last, one, 0)
+
+    def send_all(source_of, target, send_sem, recv_sem, first=1, last=n):
+        if first == 1:
+            pltpu.make_async_copy(source_of(me), target, recv_sem).start()
+
+        def send(to):
             pltpu.make_async_remote_copy(
                 src_ref=source_of(to),
                 dst_ref=target,
@@ -263,9 +280,8 @@
                 device_id={"dp": side, "seq": to},
                 device_id_type=MESH,
             ).start()
-            return carry
-
-        lax.fori_loop(1, n, one, 0)
+
+        for_peers(first, last, send)
 
     def wait_bytes(ref, sem):
         pltpu.make_async_copy(ref, ref, sem).wait()
@@ -278,8 +294,7 @@
         filter_source(me), filter_all.at[side, me, my_half, :], filter_got
     ).start()
 
-    def send_filter(k, carry):
-        to = lax.rem(me + k, n)
+    def send_filter(to):
         start = pl.multiple_of(lax.rem(to, 2) * half, half)
         pltpu.make_async_remote_copy(
             src_ref=filter_source(to),
@@ -289,9 +304,8 @@
             device_id={"dp": side, "seq": to},
             device_id_type=MESH,
         ).start()
-        return carry
-
-    lax.fori_loop(1, n, send_filter, 0)
+
+    for_peers(1, n, send_filter)
     send_all(
         lambda to: signal_ref.at[lax.div(to, 2), lax.rem(to, 2)],
         signal_all.at[my_rows, :],
@@ -405,45 +419,53 @@
                 back_imaginary * real - back_real * imaginary,
             )
         ):
-            values = values.reshape(per_chunk, rows, size)
-            terms_wide[part, blocks] = values
-            terms[part, blocks] = values.astype(jnp.bfloat16)
+            terms_wide[part, blocks] = values.reshape(per_chunk, rows, size)
 
     loop(transform_and_terms)
-    terms_copies = []
-    for i, (to_side, to_seq) in enumerate(partners):
-        start = pl.multiple_of(lax.rem(to_seq, 2) * half, half)
-        terms_copies.append(
-            pltpu.make_async_remote_copy(
-                src_ref=terms.at[to_side, :, pl.ds(start, half), :],
-                dst_ref=terms_got.at[i],
-                send_sem=terms_send.at[i],
-                recv_sem=terms_recv.at[i],
-                device_id={"dp": to_side, "seq": to_seq},
-                device_id_type=MESH,
-            )
-        )
-    for copy in terms_copies:
-        copy.start()
+    mate_half = pl.ds(pl.multiple_of(half - channel * half, half), half)
+    mate_copy = pltpu.make_async_remote_copy(
+        src_ref=terms_wide.at[:, :, mate_half, :],
+        dst_ref=terms_mate,
+        send_sem=mate_send,
+        recv_sem=mate_got,
+        device_id={"dp": side, "seq": mate},
+        device_id_type=MESH,
+    )
+    mate_copy.start()
 
     loop(lambda i: filtered(cotangent_spec, -1.0, i))
+    mate_copy.wait()
+    terms_out[...] = (terms_wide[other, :, my_half, :] + terms_mate[other]).astype(jnp.bfloat16)
+    terms_copy = pltpu.make_async_remote_copy(
+        src_ref=terms_out,
+        dst_ref=terms_got,
+        send_sem=terms_send,
+        recv_sem=terms_recv,
+        device_id={"dp": other, "seq": me},
+        device_id_type=MESH,
+    )
+    terms_copy.start()
     loop(lambda i: restored(grad_all, i))
-    send_all(
-        lambda to: rows_of(grad_all, to), grad_signal_ref.at[group, channel], grad_send, grad_got
-    )
-
-    for copy in terms_copies:
-        copy.wait()
-    total = terms_wide[side, :, my_half, :]
-    for i in range(3):
-        total = total + terms_got[i].astype(jnp.float32)
-    grad_part[...] = total.astype(jnp.bfloat16)
+    send_grad = functools.partial(
+        send_all,
+        lambda to: rows_of(grad_all, to),
+        grad_signal_ref.at[group, channel],
+        grad_send,
+        grad_got,
+    )
+    send_grad(1, across)
+
+    terms_copy.wait()
+    grad_part[...] = (
+        terms_wide[side, :, my_half, :] + terms_mate[side] + terms_got[...].astype(jnp.float32)
+    ).astype(jnp.bfloat16)
     send_all(
         lambda to: grad_part.at[to],
         grad_filter_ref.at[side, group, my_half, :],
         part_send,
         part_got,
     )
+    send_grad(across, n)
     wait_bytes(grad_filter_ref.at[side], part_got)
     swap = pltpu.make_async_remote_copy(
         src_ref=grad_filter_ref.at[side],
@@ -481,7 +503,7 @@
         out_shape=tuple(
             jax.ShapeDtypeStruct(x.shape, x.dtype) for x in (signal, cotangent, filter_spec)
         ),
-        in_specs=[anywhere] * 7,
+        in_specs=[pl.BlockSpec(memory_space=pltpu.HBM)] * 7,
         out_specs=(anywhere,) * 3,
         scratch_shapes=[
             pltpu.VMEM((size, size), bf16),
@@ -497,8 +519,9 @@
             pltpu.VMEM((size, size), bf16),
             pltpu.VMEM((size, size), bf16),
             pltpu.VMEM((2, n, rows, size), f32),
-            pltpu.VMEM((2, n, rows, size), bf16),
-            pltpu.VMEM((3, n, half, size), bf16),
+            pltpu.VMEM((2, n, half, size), f32),
+            pltpu.VMEM((n, half, size), bf16),
+            pltpu.VMEM((n, half, size), bf16),
             pltpu.VMEM((n, half, size), bf16),
             pltpu.SemaphoreType.DMA((4,)),
             one_sem,
@@ -506,11 +529,9 @@
             three,
             three,
         ]
-        + [one_sem] * 8
-        + [three, three]
-        + [one_sem] * 4,
+        + [one_sem] * 16,
         compiler_params=pltpu.CompilerParams(
-            collective_id=0, has_side_effects=True, vmem_limit_bytes=44 * 1024 * 1024
+            collective_id=0, has_side_effects=True, vmem_limit_bytes=60 * 1024 * 1024
         ),
         cost_estimate=pl.CostEstimate(
             flops=24 * size**3 * 2, bytes_accessed=12 * size * size * 2, transcendentals=0

time: 85 us -> 73.6 us (0.87)
  local copies, waits for them, and re-layouts: 11.1 us -> 4.62 us
  Pallas kernels: 72.7 us -> 68.2 us
    unnamed x17 -> x5, local copies, waits for them, and re-layouts: 11.1 us -> 4.62 us
    pallas_call x1, Pallas kernels: 72.7 us -> 68.2 us  [whole_body(): pl.pallas_call(functools.partial(whole_kernel, n), out_shape=tuple((jax.S...]
where the time goes in v2:
time: 73.6 us; the launch traced here: 73.5 us
  Pallas kernels  68.2 us (93%)
  local copies, waits for them, and re-layouts  4.62 us (6%)
    pallas_call x1, Pallas kernels, whole_body(): pl.pallas_call(functools.partial(whole_kernel, n), out_shape=tuple((jax.S...  68.2 us
    unnamed x5, local copies, waits for them, and re-layouts  4.62 us

profile of v2, /device:TPU:0, one launch (start us, length us, event | category | flops | bytes accessed | tf_op | source)
XLA Modules:
  0.0 73.5 jit_solution(6456300165256215138)
XLA Ops:
  0.6 68.2 %shard_map.94 = (bf16[8,2,32,512]{3,2,1,0:T(8,128)(2,1)}, bf16[8,2,32,512]{3,2,1,0:T(8,128)(2,1)}, bf16[2,8,32,512]{3,2,1,0:T(8,128)(2,1)}) custom-call(bf16[8,2,32,512]{3,2,1,0:T(8,128)(2,1)} %signal_ref.1, bf16[8,2,32,512]{3,2,1,0:T(8,128)(2,1)} %cotangent_ref.1, bf16[2,8,32,512]{3,2,1,0:T(8,128)(2,1)} %filter_ref.1, ...), custom_call_target="tpu_custom_call" | custom-call | flops 6442450944 | bytes 6291456 | tf_op jit(solution)/shard_map/pallas_call | solution.py:501
  68.8 0.0 copy-start
  68.8 1.9 %copy.13 = bf16[8,2,32,512]{3,2,1,0:T(8,128)(2,1)} copy(bf16[8,2,32,512]{3,2,1,0:T(8,128)(2,1)} %get-tuple-element.6) | data formatting | bytes 1048576
  70.8 1.9 %copy.14 = bf16[8,2,32,512]{3,2,1,0:T(8,128)(2,1)} copy(bf16[8,2,32,512]{3,2,1,0:T(8,128)(2,1)} %get-tuple-element.7) | data formatting | bytes 1048576
  72.7 0.0 copy-done
  72.7 0.8 %copy.15 = bf16[2,8,32,512]{3,2,1,0:T(8,128)(2,1)} copy(bf16[2,8,32,512]{3,2,1,0:T(8,128)(2,1)S(1)} %copy-done) | data formatting | bytes 1048576
Async XLA Ops:
  68.8 3.8 %copy-start = (bf16[2,8,32,512]{3,2,1,0:T(8,128)(2,1)S(1)}, bf16[2,8,32,512]{3,2,1,0:T(8,128)(2,1)}, u32[]{:S(2)}) copy-start(bf16[2,8,32,512]{3,2,1,0:T(8,128)(2,1)} %get-tuple-element.8) | copy-start | bytes 1572868

commit v3 on v2

--- a/solution.py
+++ b/solution.py
@@ -312,28 +312,37 @@
         signal_send,
         signal_got,
     )
+
+    my_quarter = filter_all.at[side, :, my_half, :]
+    wait_bytes(my_quarter, filter_got)
+    other_quarter = filter_all.at[other, :, my_half, :]
+    share_copies = [
+        pltpu.make_async_remote_copy(
+            src_ref=quarter,
+            dst_ref=quarter,
+            send_sem=share_send.at[i],
+            recv_sem=share_got.at[i],
+            device_id={"dp": to_side, "seq": to_seq},
+            device_id_type=MESH,
+        )
+        for i, (quarter, to_side, to_seq) in enumerate(
+            (
+                (my_quarter, other, me),
+                (my_quarter, side, mate),
+                (other_quarter, side, mate),
+            )
+        )
+    ]
+    share_copies[0].start()
+    share_copies[1].start()
     send_all(
         lambda to: cotangent_ref.at[lax.div(to, 2), lax.rem(to, 2)],
         cotangent_all.at[my_rows, :],
         cotangent_send,
         cotangent_got,
     )
-
-    my_quarter = filter_all.at[side, :, my_half, :]
-    wait_bytes(my_quarter, filter_got)
-    share_copies = [
-        pltpu.make_async_remote_copy(
-            src_ref=my_quarter,
-            dst_ref=my_quarter,
-            send_sem=share_send.at[i],
-            recv_sem=share_got.at[i],
-            device_id={"dp": to_side, "seq": to_seq},
-            device_id_type=MESH,
-        )
-        for i, (to_side, to_seq) in enumerate(partners)
-    ]
-    for copy in share_copies:
-        copy.start()
+    share_copies[0].wait_recv()
+    share_copies[2].start()
 
     for copy in table_copies:
         copy.wait()
@@ -397,8 +406,9 @@
 
     wait_bytes(signal_all, signal_got)
     loop(lambda i: transform(signal_all, signal_spec, i))
-    for copy in share_copies:
-        copy.wait()
+    share_copies[0].wait_send()
+    share_copies[1].wait()
+    share_copies[2].wait()
     loop(lambda i: filtered(signal_spec, 1.0, i))
     loop(lambda i: restored(output_all, i))
     send_all(
@@ -489,6 +499,30 @@
     wait_bytes(grad_part.at[pl.ds(0, n - 1)], part_send)
 
 
+DEPTH = 2
+
+
+def hand_over_kernel(a_in, b_in, c_in, a_out, b_out, c_out, a_held, b_held, c_held, read, wrote):
+    reads, writes = [], []
+    for source, target, held in (
+        (a_in, a_out, a_held),
+        (b_in, b_out, b_held),
+        (c_in, c_out, c_held),
+    ):
+        part = source.shape[0] // DEPTH
+        for i in range(DEPTH):
+            at, sem = pl.ds(i * part, part), len(reads)
+            reads.append(pltpu.make_async_copy(source.at[at], held.at[at], read.at[sem]))
+            writes.append(pltpu.make_async_copy(held.at[at], target.at[at], wrote.at[sem]))
+    for copy in reads:
+        copy.start()
+    for before, after in zip(reads, writes):
+        before.wait()
+        after.start()
+    for copy in writes:
+        copy.wait()
+
+
 def whole_body(n, signal, cotangent, filter_spec):
     size = signal.shape[3]
     rows = signal.shape[2]
@@ -498,7 +532,7 @@
     anywhere = pl.BlockSpec(memory_space=pl.ANY)
     one_sem = pltpu.SemaphoreType.DMA(())
     three = pltpu.SemaphoreType.DMA((3,))
-    return pl.pallas_call(
+    landed = pl.pallas_call(
         functools.partial(whole_kernel, n),
         out_shape=tuple(
             jax.ShapeDtypeStruct(x.shape, x.dtype) for x in (signal, cotangent, filter_spec)
@@ -537,6 +571,19 @@
             flops=24 * size**3 * 2, bytes_accessed=12 * size * size * 2, transcendentals=0
         ),
     )(signal, cotangent, filter_spec, *tables)
+    pieces = 3 * DEPTH
+    return pl.pallas_call(
+        hand_over_kernel,
+        out_shape=tuple(jax.ShapeDtypeStruct(x.shape, x.dtype) for x in landed),
+        in_specs=[anywhere] * 3,
+        out_specs=(anywhere,) * 3,
+        scratch_shapes=[pltpu.VMEM(x.shape, x.dtype) for x in landed]
+        + [pltpu.SemaphoreType.DMA((pieces,))] * 2,
+        compiler_params=pltpu.CompilerParams(vmem_limit_bytes=60 * 1024 * 1024),
+        cost_estimate=pl.CostEstimate(
+            flops=0, bytes_accessed=12 * rows * n * size, transcendentals=0
+        ),
+    )(*landed)
 
 
 def solution(mesh):

time: 73.6 us -> 71.2 us (0.967)
  local copies, waits for them, and re-layouts: 4.62 us -> 0 us
  Pallas kernels: 68.2 us -> 70.4 us
    unnamed x5 -> x0, local copies, waits for them, and re-layouts: 4.62 us -> none
    pallas_call x0 -> x1, Pallas kernels: none -> 2.19 us  [whole_body(): pl.pallas_call(hand_over_kernel, out_shape=tuple((jax.ShapeDtypeStruct(x....]
where the time goes in v3:
time: 71.2 us; the launch traced here: 71 us
  Pallas kernels  70.4 us (99%)
    pallas_call x1, Pallas kernels, whole_body(): pl.pallas_call(functools.partial(whole_kernel, n), out_shape=tuple((jax.S...  68.2 us
    pallas_call x1, Pallas kernels, whole_body(): pl.pallas_call(hand_over_kernel, out_shape=tuple((jax.ShapeDtypeStruct(x....  2.19 us

profile of v3, /device:TPU:0, one launch (start us, length us, event | category | flops | bytes accessed | tf_op | source)
XLA Modules:
  0.0 71.0 jit_solution(2920402747447351168)
XLA Ops:
  0.6 68.2 %shard_map.94 = (bf16[8,2,32,512]{3,2,1,0:T(8,128)(2,1)}, bf16[8,2,32,512]{3,2,1,0:T(8,128)(2,1)}, bf16[2,8,32,512]{3,2,1,0:T(8,128)(2,1)}) custom-call(bf16[8,2,32,512]{3,2,1,0:T(8,128)(2,1)} %signal_ref.1, bf16[8,2,32,512]{3,2,1,0:T(8,128)(2,1)} %cotangent_ref.1, bf16[2,8,32,512]{3,2,1,0:T(8,128)(2,1)} %filter_ref.1, ...), custom_call_target="tpu_custom_call" | custom-call | flops 6442450944 | bytes 6291456 | tf_op jit(solution)/shard_map/pallas_call | solution.py:535
  68.8 2.2 %shard_map.95 = (bf16[8,2,32,512]{3,2,1,0:T(8,128)(2,1)}, bf16[8,2,32,512]{3,2,1,0:T(8,128)(2,1)}, bf16[2,8,32,512]{3,2,1,0:T(8,128)(2,1)}) custom-call(bf16[8,2,32,512]{3,2,1,0:T(8,128)(2,1)} %get-tuple-element.6.a_in, bf16[8,2,32,512]{3,2,1,0:T(8,128)(2,1)} %get-tuple-element.7.b_in, bf16[2,8,32,512]{3,2,1,0:T(8,128)(2,1)} %get-tuple-element.8.c_in), custom_call_target="tpu_custom_call" | custom-call | bytes 3145728 | tf_op jit(solution)/shard_map/pallas_call | solution.py:575

commit v4 on v3

--- a/solution.py
+++ b/solution.py
@@ -211,8 +211,8 @@
     size = signal_all.shape[0]
     rows = size // n
     half = rows // 2
-    chunk = 256
-    chunks = size // chunk
+    chunks = 2
+    chunk = size // chunks
     per_chunk = chunk // rows
     me = lax.axis_index("seq")
     side = lax.axis_index("dp")
@@ -335,12 +335,15 @@
     ]
     share_copies[0].start()
     share_copies[1].start()
-    send_all(
+    send_cotangent = functools.partial(
+        send_all,
         lambda to: cotangent_ref.at[lax.div(to, 2), lax.rem(to, 2)],
         cotangent_all.at[my_rows, :],
         cotangent_send,
         cotangent_got,
     )
+    early = max(2, n // 3)
+    send_cotangent(1, early)
     share_copies[0].wait_recv()
     share_copies[2].start()
 
@@ -390,9 +393,24 @@
     def restored(result, i):
         at = pl.ds(pl.multiple_of(i * chunk, chunk), chunk)
         turned = jnp.dot(
-            forward_table[at, :], middle[...], preferred_element_type=jnp.float32
-        )
-        result[:, at] = turned.T.astype(jnp.bfloat16)
+            forward_table[:size, :], middle[:, at], preferred_element_type=jnp.float32
+        )
+        result[at, :] = turned.T.astype(jnp.bfloat16)
+
+    def send_rows(result, target, send_sem, recv_sem, part, first, last):
+        def one(k, carry):
+            to = part * across + lax.rem(place + k, across)
+            pltpu.make_async_remote_copy(
+                src_ref=rows_of(result, to),
+                dst_ref=target,
+                send_sem=send_sem,
+                recv_sem=recv_sem,
+                device_id={"dp": side, "seq": to},
+                device_id_type=MESH,
+            ).start()
+            return carry
+
+        lax.fori_loop(first, last, one, 0)
 
     def loop(fn):
         def one(i, carry):
@@ -405,15 +423,23 @@
         return ref.at[pl.ds(pl.multiple_of(to * rows, rows), rows), :]
 
     wait_bytes(signal_all, signal_got)
+    send_cotangent(early, n)
     loop(lambda i: transform(signal_all, signal_spec, i))
     share_copies[0].wait_send()
     share_copies[1].wait()
     share_copies[2].wait()
     loop(lambda i: filtered(signal_spec, 1.0, i))
-    loop(lambda i: restored(output_all, i))
-    send_all(
-        lambda to: rows_of(output_all, to), output_ref.at[group, channel], output_send, output_got
-    )
+    there = 1 - my_part
+    send_output = functools.partial(
+        send_rows, output_all, output_ref.at[group, channel], output_send, output_got
+    )
+    restored(output_all, there)
+    send_output(there, 0, across)
+    restored(output_all, my_part)
+    send_output(my_part, 1, across)
+    pltpu.make_async_copy(
+        rows_of(output_all, me), output_ref.at[group, channel], output_got
+    ).start()
 
     wait_bytes(cotangent_all, cotangent_got)
 
@@ -455,15 +481,15 @@
         device_id_type=MESH,
     )
     terms_copy.start()
-    loop(lambda i: restored(grad_all, i))
     send_grad = functools.partial(
-        send_all,
-        lambda to: rows_of(grad_all, to),
-        grad_signal_ref.at[group, channel],
-        grad_send,
-        grad_got,
-    )
-    send_grad(1, across)
+        send_rows, grad_all, grad_signal_ref.at[group, channel], grad_send, grad_got
+    )
+    restored(grad_all, there)
+    send_grad(there, 0, across // 2)
+    restored(grad_all, my_part)
+    pltpu.make_async_copy(
+        rows_of(grad_all, me), grad_signal_ref.at[group, channel], grad_got
+    ).start()
 
     terms_copy.wait()
     grad_part[...] = (
@@ -475,7 +501,8 @@
         part_send,
         part_got,
     )
-    send_grad(across, n)
+    send_grad(there, across // 2, across)
+    send_grad(my_part, 1, across)
     wait_bytes(grad_filter_ref.at[side], part_got)
     swap = pltpu.make_async_remote_copy(
         src_ref=grad_filter_ref.at[side],

time: 71.2 us -> 77 us (1.081)
  Pallas kernels: 70.4 us -> 76.2 us
    pallas_call x1, Pallas kernels: 68.2 us -> 74.1 us  [whole_body(): pl.pallas_call(functools.partial(whole_kernel, n), out_shape=tuple((jax.S...]
where the time goes in v4:
time: 77 us; the launch traced here: 76.9 us
  Pallas kernels  76.2 us (99%)
    pallas_call x1, Pallas kernels, whole_body(): pl.pallas_call(functools.partial(whole_kernel, n), out_shape=tuple((jax.S...  74.1 us
    pallas_call x1, Pallas kernels, whole_body(): pl.pallas_call(hand_over_kernel, out_shape=tuple((jax.ShapeDtypeStruct(x....  2.19 us

profile of v4, /device:TPU:0, one launch (start us, length us, event | category | flops | bytes accessed | tf_op | source)
XLA Modules:
  0.0 76.9 jit_solution(6579893062907091790)
XLA Ops:
  0.6 74.1 %shard_map.94 = (bf16[8,2,32,512]{3,2,1,0:T(8,128)(2,1)}, bf16[8,2,32,512]{3,2,1,0:T(8,128)(2,1)}, bf16[2,8,32,512]{3,2,1,0:T(8,128)(2,1)}) custom-call(bf16[8,2,32,512]{3,2,1,0:T(8,128)(2,1)} %signal_ref.1, bf16[8,2,32,512]{3,2,1,0:T(8,128)(2,1)} %cotangent_ref.1, bf16[2,8,32,512]{3,2,1,0:T(8,128)(2,1)} %filter_ref.1, ...), custom_call_target="tpu_custom_call" | custom-call | flops 6442450944 | bytes 6291456 | tf_op jit(solution)/shard_map/pallas_call | solution.py:562
  74.7 2.2 %shard_map.95 = (bf16[8,2,32,512]{3,2,1,0:T(8,128)(2,1)}, bf16[8,2,32,512]{3,2,1,0:T(8,128)(2,1)}, bf16[2,8,32,512]{3,2,1,0:T(8,128)(2,1)}) custom-call(bf16[8,2,32,512]{3,2,1,0:T(8,128)(2,1)} %get-tuple-element.6.a_in, bf16[8,2,32,512]{3,2,1,0:T(8,128)(2,1)} %get-tuple-element.7.b_in, bf16[2,8,32,512]{3,2,1,0:T(8,128)(2,1)} %get-tuple-element.8.c_in), custom_call_target="tpu_custom_call" | custom-call | bytes 3145728 | tf_op jit(solution)/shard_map/pallas_call | solution.py:602

commit v5 on v3

--- a/solution.py
+++ b/solution.py
@@ -395,11 +395,8 @@
         result[:, at] = turned.T.astype(jnp.bfloat16)
 
     def loop(fn):
-        def one(i, carry):
+        for i in range(chunks):
             fn(i)
-            return carry
-
-        lax.fori_loop(0, chunks, one, 0)
 
     def rows_of(ref, to):
         return ref.at[pl.ds(pl.multiple_of(to * rows, rows), rows), :]

time: 71.2 us -> 72.2 us (1.014)
  Pallas kernels: 70.4 us -> 71.2 us
    pallas_call x1, Pallas kernels: 68.2 us -> 69 us  [whole_body(): pl.pallas_call(functools.partial(whole_kernel, n), out_shape=tuple((jax.S...]
where the time goes in v5:
time: 72.2 us; the launch traced here: 71.8 us
  Pallas kernels  71.2 us (99%)
    pallas_call x1, Pallas kernels, whole_body(): pl.pallas_call(functools.partial(whole_kernel, n), out_shape=tuple((jax.S...  69 us
    pallas_call x1, Pallas kernels, whole_body(): pl.pallas_call(hand_over_kernel, out_shape=tuple((jax.ShapeDtypeStruct(x....  2.19 us

profile of v5, /device:TPU:0, one launch (start us, length us, event | category | flops | bytes accessed | tf_op | source)
XLA Modules:
  0.0 71.8 jit_solution(1626605816105944698)
XLA Ops:
  0.6 69.0 %shard_map.94 = (bf16[8,2,32,512]{3,2,1,0:T(8,128)(2,1)}, bf16[8,2,32,512]{3,2,1,0:T(8,128)(2,1)}, bf16[2,8,32,512]{3,2,1,0:T(8,128)(2,1)}) custom-call(bf16[8,2,32,512]{3,2,1,0:T(8,128)(2,1)} %signal_ref.1, bf16[8,2,32,512]{3,2,1,0:T(8,128)(2,1)} %cotangent_ref.1, bf16[2,8,32,512]{3,2,1,0:T(8,128)(2,1)} %filter_ref.1, ...), custom_call_target="tpu_custom_call" | custom-call | flops 6442450944 | bytes 6291456 | tf_op jit(solution)/shard_map/pallas_call | solution.py:532
  69.6 2.2 %shard_map.95 = (bf16[8,2,32,512]{3,2,1,0:T(8,128)(2,1)}, bf16[8,2,32,512]{3,2,1,0:T(8,128)(2,1)}, bf16[2,8,32,512]{3,2,1,0:T(8,128)(2,1)}) custom-call(bf16[8,2,32,512]{3,2,1,0:T(8,128)(2,1)} %get-tuple-element.6.a_in, bf16[8,2,32,512]{3,2,1,0:T(8,128)(2,1)} %get-tuple-element.7.b_in, bf16[2,8,32,512]{3,2,1,0:T(8,128)(2,1)} %get-tuple-element.8.c_in), custom_call_target="tpu_custom_call" | custom-call | bytes 3145728 | tf_op jit(solution)/shard_map/pallas_call | solution.py:572
